TPU v7x, 128 devices: a whole 4x4x4 slice. The times are simulated.
128 devices in a mesh: sub: 8 (over x, core), band: 16 (over z, y).
Axes of the slice: x: 4, y: 4, z: 4, core: 2. Of those that a mesh axis runs over, the one named last changes fastest.
Arguments:
- coeffs_in: float32 [32, 128, 1024], P('sub'), may hold values from -6 to 6
- basis: bfloat16 [224, 32], P('band'), may hold values from -0.375 to 0.375
- kernels: float32 [224, 9, 9], P('band'), may hold values from -0.625 to 0.625
- response: bfloat16 [8, 224], P(None, 'band'), may hold values from -1.5 to 1.5
- hs_image: bfloat16 [224, 32, 256], P('band', 'sub'), may hold values from -6 to 6
- ms_image: bfloat16 [8, 128, 1024], P(None, 'sub'), may hold values from -6 to 6
Outputs:
- coeffs: float32 [32, 128, 1024], P('sub')
All inputs are finite; a program needn't handle non-finite values.
Results may differ from a plain program's by a relative error of at most 0.0003.
The roundings to bfloat16 on the way count: a program that leaves them out, or rounds other values in their place, can miss the bound.
Values may be sent and summed in bfloat16 or wider, within the bound.
No kernel may reach another device: no remote copies, remote signals or barrier semaphores. Data moves between devices by JAX's collectives and lax.ppermute only.
A program may use at most 128 MiB of HBM per device.

v0:
```python
import jax
import jax.numpy as jnp
from jax import lax
from jax.sharding import PartitionSpec as P

ITERS = 2
step_scale = 0.15


def padded_2(cells, sides, width):
    for axis, dim in sides:
        count = lax.axis_size(axis)
        ends = count - 1
        head = lax.slice_in_dim(cells, 0, width, axis=dim)
        tail = lax.slice_in_dim(cells, cells.shape[dim] - width, cells.shape[dim], axis=dim)
        cells = jnp.concatenate(
            [
                lax.ppermute(tail, axis, [(i, (i + 1) % count) for i in range(ends)]),
                cells,
                lax.ppermute(head, axis, [((i + 1) % count, i) for i in range(ends)]),
            ],
            axis=dim,
        )
    return cells


def hs_gradient(rounded, basis, kernels, hs_image):
    chans, rows, width = rounded.shape
    bands = basis.shape[0]
    groups = rows // 4
    columns = width // 4
    mixed = jnp.dot(basis, rounded.reshape(chans, -1), preferred_element_type=jnp.float32).astype(
        jnp.bfloat16
    )
    mixed = mixed.reshape(bands, rows, width)
    extended = padded_2(mixed, (("sub", 1),), 4)
    padded = jnp.pad(extended, ((0, 0), (0, 0), (4, 4)))
    phases = padded.reshape(bands, groups + 2, 4, columns + 2, 4).transpose(0, 2, 4, 1, 3)
    blurred = jnp.zeros((bands, groups, columns), jnp.float32)
    for row_tap in range(9):
        row_step, row_phase = divmod(row_tap, 4)
        for col_tap in range(9):
            col_step, col_phase = divmod(col_tap, 4)
            window = phases[
                :, row_phase, col_phase, row_step : row_step + groups, col_step : col_step + columns
            ]
            blurred = blurred + kernels[:, row_tap, col_tap][:, None, None] * window
    misfit = hs_image.astype(jnp.float32) - blurred
    misfit_ext = padded_2(misfit, (("sub", 1),), 1)
    misfit_pad = jnp.pad(misfit_ext, ((0, 0), (0, 0), (1, 1)))
    outer = []
    for row_phase in range(4):
        inner = []
        for col_phase in range(4):
            total = jnp.zeros((bands, groups, columns), jnp.float32)
            for row_step in range(3):
                if 4 * row_step + row_phase > 8:
                    continue
                for col_step in range(3):
                    if 4 * col_step + col_phase > 8:
                        continue
                    weight = kernels[:, 4 * row_step + row_phase, 4 * col_step + col_phase][
                        :, None, None
                    ]
                    window = misfit_pad[
                        :,
                        2 - row_step : 2 - row_step + groups,
                        2 - col_step : 2 - col_step + columns,
                    ]
                    total = total + weight * window
            inner.append(total)
        outer.append(jnp.stack(inner, axis=1))
    back = jnp.stack(outer, axis=1).transpose(0, 3, 1, 4, 2).reshape(bands, rows * width)
    back = back.astype(jnp.bfloat16)
    grad = jnp.einsum("lk,lp->kp", basis, back, preferred_element_type=jnp.float32)
    return grad.reshape(chans, rows, width)


def ms_gradient(rounded, ms_rows, combined):
    chans, rows, width = rounded.shape
    sensors = ms_rows.shape[0]
    predicted = jnp.dot(combined, rounded.reshape(chans, -1), preferred_element_type=jnp.float32)
    ms_misfit = (ms_rows.reshape(sensors, -1).astype(jnp.float32) - predicted).astype(jnp.bfloat16)
    grad = jnp.einsum("mk,mp->kp", combined, ms_misfit, preferred_element_type=jnp.float32)
    return grad.reshape(chans, rows, width)


def per_device(coeffs_in, basis, kernels, response, hs_image, ms_image):
    partial_map = jnp.dot(response, basis, preferred_element_type=jnp.float32)
    combined = lax.psum(partial_map, "band").astype(jnp.bfloat16)
    current = coeffs_in
    for turn in range(ITERS):
        rounded = lax.all_to_all(
            current.astype(jnp.bfloat16), "sub", split_axis=1, concat_axis=0, tiled=True
        )
        hs_part = hs_gradient(rounded, basis, kernels, hs_image)
        hs_total = lax.psum(hs_part, "band")
        update = step_scale * (hs_total + ms_gradient(rounded, ms_image, combined))
        current = current + lax.all_to_all(update, "sub", split_axis=0, concat_axis=1, tiled=True)
    return current


def solution(mesh):
    return jax.shard_map(
        per_device,
        mesh=mesh,
        in_specs=(
            P("sub", None, None),
            P("band", None),
            P("band", None, None),
            P(None, "band"),
            P("band", "sub", None),
            P(None, "sub", None),
        ),
        out_specs=P("sub", None, None),
        check_vma=False,
    )
```

profile of v0, /device:TPU:1, one launch (start us, length us, event | category | flops | bytes accessed | tf_op | source)
XLA Modules:
  0.0 448.3 jit_solution(3410588063902400602)
XLA Ops:
  6.5 3.9 copy.459
  10.5 5.8 %all-to-all-start = ((bf16[4,128,1024]{2,0,1:T(4,128)(2,1)}), bf16[4,128,1024]{2,0,1:T(4,128)(2,1)S(1)}, u32[]{:S(2)}, u32[]{:S(2)}) async-start(bf16[4,128,1024]{2,0,1:T(4,128)(2,1)} %copy.459), calls=%async_computation | async-start | bytes 2097152 | tf_op jit(solution)/shard_map/all_to_all | solution.py:93
  19.6 11.8 %all-to-all-done = bf16[4,128,1024]{2,0,1:T(4,128)(2,1)S(1)} async-done(((bf16[4,128,1024]{2,0,1:T(4,128)(2,1)}), bf16[4,128,1024]{2,0,1:T(4,128)(2,1)S(1)}, u32[]{:S(2)}, u32[]{:S(2)}) %all-to-all-start) | async-done | bytes 1048608 | tf_op jit(solution)/shard_map/all_to_all | solution.py:93
  42.4 4.8 %copy.442 = bf16[14,24,1024]{0,2,1:T(8,128)(2,1)} copy(bf16[14,24,1024]{2,1,0:T(8,128)(2,1)S(1)} %pad_maximum_fusion) | data formatting | bytes 1376256
  47.2 7.5 %pad.14.clone = bf16[14,24,1032]{0,2,1:T(8,128)(2,1)} pad(bf16[14,24,1024]{0,2,1:T(8,128)(2,1)} %copy.442, bf16[]{:T(256)} %constant.4.clone.1), padding=0_0x0_0x4_4 | pad | bytes 1381634 | tf_op jit(solution)/shard_map/jit(_pad)/pad | solution.py:37
  54.7 11.1 %copy.392 = bf16[14,6,4,258,4]{3,1,0,4,2:T(8,128)(2,1)S(1)} copy(bf16[14,6,4,258,4]{0,4,3,2,1:T(4,128)(2,1)} %bitcast.1049) | data formatting | bytes 1387008 | tf_op jit(solution)/shard_map/reshape | solution.py:38
  65.8 3.8 convert_subtract_fusion.1
  86.3 4.9 %copy.413 = bf16[14,4,4,256,4]{0,4,3,2,1:T(4,128)(2,1)} copy(bf16[14,4,4,256,4]{3,1,4,2,0:T(4,128)(2,1)S(1)} %maximum_bitcast_fusion) | data formatting | bytes 917504 | tf_op jit(solution)/shard_map/convert_element_type | solution.py:74
  91.2 3.7 fusion.212
  98.9 35.0 %psum.22 = bf16[8,32]{1,0:T(8,128)(2,1)S(1)} all-reduce(f32[8,32]{1,0:T(8,128)S(1)} %fusion.213), channel_id=1, replica_groups=mesh['sub'=8,'band'=16] {'band'}, use_global_device_ids=true, to_apply=%region_1.2 | all-reduce | flops 256 | bytes 1536 | tf_op jit(solution)/shard_map/psum | solution.py:90
  138.5 49.5 %all-reduce.7.cloned.1.call-done = f32[32,16,1024]{2,1,0:T(8,128)} async-done(((f32[32,16,1024]{2,1,0:T(8,128)}), f32[32,16,1024]{2,1,0:T(8,128)}) %all-reduce.7.cloned.1.call-update) | async-done | bytes 2097168 | tf_op jit(solution)/shard_map/psum | solution.py:97
  189.9 32.4 %all_to_all.66 = f32[32,16,1024]{2,1,0:T(8,128)S(1)} all-to-all(f32[32,16,1024]{2,1,0:T(8,128)S(1)} %fusion.3), channel_id=1, replica_groups=mesh['sub'=8,'band'=16] {'sub'}, dimensions={0} | all-to-all | bytes 4194304 | tf_op jit(solution)/shard_map/all_to_all | solution.py:99
  225.7 18.5 %all_to_all.67 = bf16[4,128,1024]{2,0,1:T(4,128)(2,1)S(1)} all-to-all(bf16[4,128,1024]{2,0,1:T(4,128)(2,1)S(1)} %fusion.6), channel_id=1, replica_groups=mesh['sub'=8,'band'=16] {'sub'}, dimensions={1} | all-to-all | bytes 2097152 | tf_op jit(solution)/shard_map/all_to_all | solution.py:93
  246.9 3.1 collective-permute-start.4
  252.0 4.1 collective-permute-done.5
  256.4 4.8 %copy.443 = bf16[14,24,1024]{0,2,1:T(8,128)(2,1)} copy(bf16[14,24,1024]{2,1,0:T(8,128)(2,1)S(1)} %pad_maximum_fusion.1) | data formatting | bytes 1376256
  261.2 7.5 %pad.16.clone = bf16[14,24,1032]{0,2,1:T(8,128)(2,1)} pad(bf16[14,24,1024]{0,2,1:T(8,128)(2,1)} %copy.443, bf16[]{:T(256)} %constant.4.clone.1), padding=0_0x0_0x4_4 | pad | bytes 1381634 | tf_op jit(solution)/shard_map/jit(_pad)/pad | solution.py:37
  268.7 11.1 %copy.418 = bf16[14,6,4,258,4]{3,1,0,4,2:T(8,128)(2,1)S(1)} copy(bf16[14,6,4,258,4]{0,4,3,2,1:T(4,128)(2,1)} %bitcast.1048) | data formatting | bytes 1387008 | tf_op jit(solution)/shard_map/reshape | solution.py:38
  280.0 4.2 convert_subtract_fusion
  301.1 4.9 %copy.439 = bf16[14,4,4,256,4]{0,4,3,2,1:T(4,128)(2,1)} copy(bf16[14,4,4,256,4]{3,1,4,2,0:T(4,128)(2,1)S(1)} %maximum_bitcast_fusion.1) | data formatting | bytes 917504 | tf_op jit(solution)/shard_map/convert_element_type | solution.py:74
  306.0 3.7 fusion.214
  316.4 4.1 copy.452
  320.5 79.2 %all-reduce.9.cloned.1.call-done = f32[32,16,1024]{2,1,0:T(8,128)} async-done(((f32[32,16,1024]{2,1,0:T(8,128)}), f32[32,16,1024]{2,1,0:T(8,128)}) %all-reduce.9.cloned.1.call-update) | async-done | bytes 2097168 | tf_op jit(solution)/shard_map/psum | solution.py:97
  402.3 32.5 %all_to_all.68 = f32[32,16,1024]{2,1,0:T(8,128)S(1)} all-to-all(f32[32,16,1024]{2,1,0:T(8,128)S(1)} %fusion.2), channel_id=1, replica_groups=mesh['sub'=8,'band'=16] {'sub'}, dimensions={0} | all-to-all | bytes 4194304 | tf_op jit(solution)/shard_map/all_to_all | solution.py:99
  (266 shorter events, 81.1 us)
Async XLA Ops:
  10.5 20.9 %all-to-all-start = ((bf16[4,128,1024]{2,0,1:T(4,128)(2,1)}), bf16[4,128,1024]{2,0,1:T(4,128)(2,1)S(1)}, u32[]{:S(2)}, u32[]{:S(2)}) async-start(bf16[4,128,1024]{2,0,1:T(4,128)(2,1)} %copy.459), calls=%async_computation | async-start | bytes 2097152 | tf_op jit(solution)/shard_map/all_to_all | solution.py:93
  16.3 171.7 %all-reduce.7.cloned.1.call-start = ((), (), s32[]{:S(2)}) async-start(), calls=%async_computation.4 | async-start | bytes 4194304 | tf_op jit(solution)/shard_map/psum | solution.py:97
  17.3 66.2 %copy-start.22 = (f32[14]{0:T(128)}, f32[14]{0:T(128)S(1)}, u32[]{:S(2)}) copy-start(f32[14]{0:T(128)S(1)} %get-tuple-element.23) | copy-start | bytes 172
  18.4 65.2 %copy-start.38 = (f32[14]{0:T(128)}, f32[14]{0:T(128)S(1)}, u32[]{:S(2)}) copy-start(f32[14]{0:T(128)S(1)} %get-tuple-element.28) | copy-start | bytes 172
  18.4 66.7 %copy-start.24 = (f32[14]{0:T(128)}, f32[14]{0:T(128)S(1)}, u32[]{:S(2)}) copy-start(f32[14]{0:T(128)S(1)} %get-tuple-element.27) | copy-start | bytes 172
  18.4 66.7 %copy-start.26 = (f32[14]{0:T(128)}, f32[14]{0:T(128)S(1)}, u32[]{:S(2)}) copy-start(f32[14]{0:T(128)S(1)} %get-tuple-element.31) | copy-start | bytes 172
  18.4 67.0 %copy-start.12 = (f32[14]{0:T(128)}, f32[14]{0:T(128)S(1)}, u32[]{:S(2)}) copy-start(f32[14]{0:T(128)S(1)} %get-tuple-element.26) | copy-start | bytes 172
  18.4 67.0 %copy-start.14 = (f32[14]{0:T(128)}, f32[14]{0:T(128)S(1)}, u32[]{:S(2)}) copy-start(f32[14]{0:T(128)S(1)} %get-tuple-element.30) | copy-start | bytes 172
  19.5 65.2 %copy-start.16 = (f32[14]{0:T(128)}, f32[14]{0:T(128)S(1)}, u32[]{:S(2)}) copy-start(f32[14]{0:T(128)S(1)} %get-tuple-element.51) | copy-start | bytes 172
  19.5 65.2 %copy-start.18 = (f32[14]{0:T(128)}, f32[14]{0:T(128)S(1)}, u32[]{:S(2)}) copy-start(f32[14]{0:T(128)S(1)} %get-tuple-element.55) | copy-start | bytes 172
  19.5 65.2 %copy-start.20 = (f32[14]{0:T(128)}, f32[14]{0:T(128)S(1)}, u32[]{:S(2)}) copy-start(f32[14]{0:T(128)S(1)} %get-tuple-element.59) | copy-start | bytes 172
  19.5 65.4 %copy-start.10 = (f32[14]{0:T(128)}, f32[14]{0:T(128)S(1)}, u32[]{:S(2)}) copy-start(f32[14]{0:T(128)S(1)} %get-tuple-element.57) | copy-start | bytes 172
  19.5 65.6 %copy-start.36 = (f32[14]{0:T(128)}, f32[14]{0:T(128)S(1)}, u32[]{:S(2)}) copy-start(f32[14]{0:T(128)S(1)} %get-tuple-element.60) | copy-start | bytes 172
  19.5 65.9 %copy-start.28 = (f32[14]{0:T(128)}, f32[14]{0:T(128)S(1)}, u32[]{:S(2)}) copy-start(f32[14]{0:T(128)S(1)} %get-tuple-element.52) | copy-start | bytes 172
  19.5 65.9 %copy-start.30 = (f32[14]{0:T(128)}, f32[14]{0:T(128)S(1)}, u32[]{:S(2)}) copy-start(f32[14]{0:T(128)S(1)} %get-tuple-element.56) | copy-start | bytes 172
  33.0 6.9 %collective-permute-start = (bf16[14,4,1024]{2,1,0:T(4,128)(2,1)S(1)}, bf16[14,4,1024]{2,1,0:T(4,128)(2,1)S(1)}, u32[]{:S(2)}, u32[]{:S(2)}) collective-permute-start(bf16[14,4,1024]{2,1,0:T(4,128)(2,1)S(1)} %get-tuple-element.88), channel_id=1, source_target_pairs={{0,16},{16,32},{32,48},{48,64},{64,80},{80,96},{96,112},{1,17},{17... | collective-permute-start | bytes 344072 | tf_op jit(solution)/shard_map/ppermute | solution.py:18
  36.0 6.1 %collective-permute-start.1 = (bf16[14,4,1024]{2,1,0:T(4,128)(2,1)S(1)}, bf16[14,4,1024]{2,1,0:T(4,128)(2,1)S(1)}, u32[]{:S(2)}, u32[]{:S(2)}) collective-permute-start(bf16[14,4,1024]{2,1,0:T(4,128)(2,1)S(1)} %get-tuple-element.89), channel_id=1, source_target_pairs={{16,0},{32,16},{48,32},{64,48},{80,64},{96,80},{112,96},{17,1},{33... | collective-permute-start | bytes 344072 | tf_op jit(solution)/shard_map/ppermute | solution.py:20
  69.6 4.9 %collective-permute-start.2 = (f32[14,1,256]{2,1,0:T(1,128)S(1)}, f32[14,1,256]{2,1,0:T(1,128)S(1)}, u32[]{:S(2)}, u32[]{:S(2)}) collective-permute-start(f32[14,1,256]{2,1,0:T(1,128)S(1)} %get-tuple-element.108), channel_id=1, source_target_pairs={{0,16},{16,32},{32,48},{48,64},{64,80},{80,96},{96,112},{1,17},{17... | collective-permute-start | bytes 43016 | tf_op jit(solution)/shard_map/ppermute | solution.py:18
  71.5 5.0 %collective-permute-start.3 = (f32[14,1,256]{2,1,0:T(1,128)S(1)}, f32[14,1,256]{2,1,0:T(1,128)S(1)}, u32[]{:S(2)}, u32[]{:S(2)}) collective-permute-start(f32[14,1,256]{2,1,0:T(1,128)S(1)} %get-tuple-element.109), channel_id=1, source_target_pairs={{16,0},{32,16},{48,32},{64,48},{80,64},{96,80},{112,96},{17,1},{33... | collective-permute-start | bytes 43016 | tf_op jit(solution)/shard_map/ppermute | solution.py:20
  97.4 302.2 %all-reduce.9.cloned.1.call-start = ((), (), s32[]{:S(2)}) async-start(), calls=%async_computation.5 | async-start | bytes 4194304 | tf_op jit(solution)/shard_map/psum | solution.py:97
  246.9 5.1 %collective-permute-start.4 = (bf16[14,4,1024]{2,1,0:T(4,128)(2,1)S(1)}, bf16[14,4,1024]{2,1,0:T(4,128)(2,1)S(1)}, u32[]{:S(2)}, u32[]{:S(2)}) collective-permute-start(bf16[14,4,1024]{2,1,0:T(4,128)(2,1)S(1)} %get-tuple-element.86), channel_id=1, source_target_pairs={{0,16},{16,32},{32,48},{48,64},{64,80},{80,96},{96,112},{1,17},{17... | collective-permute-start | bytes 344072 | tf_op jit(solution)/shard_map/ppermute | solution.py:18
  250.0 6.1 %collective-permute-start.5 = (bf16[14,4,1024]{2,1,0:T(4,128)(2,1)S(1)}, bf16[14,4,1024]{2,1,0:T(4,128)(2,1)S(1)}, u32[]{:S(2)}, u32[]{:S(2)}) collective-permute-start(bf16[14,4,1024]{2,1,0:T(4,128)(2,1)S(1)} %get-tuple-element.87), channel_id=1, source_target_pairs={{16,0},{32,16},{48,32},{64,48},{80,64},{96,80},{112,96},{17,1},{33... | collective-permute-start | bytes 344072 | tf_op jit(solution)/shard_map/ppermute | solution.py:20
  284.4 4.6 %collective-permute-start.6 = (f32[14,1,256]{2,1,0:T(1,128)S(1)}, f32[14,1,256]{2,1,0:T(1,128)S(1)}, u32[]{:S(2)}, u32[]{:S(2)}) collective-permute-start(f32[14,1,256]{2,1,0:T(1,128)S(1)} %get-tuple-element.106), channel_id=1, source_target_pairs={{0,16},{16,32},{32,48},{48,64},{64,80},{80,96},{96,112},{1,17},{17... | collective-permute-start | bytes 43016 | tf_op jit(solution)/shard_map/ppermute | solution.py:18
  286.3 5.0 %collective-permute-start.7 = (f32[14,1,256]{2,1,0:T(1,128)S(1)}, f32[14,1,256]{2,1,0:T(1,128)S(1)}, u32[]{:S(2)}, u32[]{:S(2)}) collective-permute-start(f32[14,1,256]{2,1,0:T(1,128)S(1)} %get-tuple-element.107), channel_id=1, source_target_pairs={{16,0},{32,16},{48,32},{64,48},{80,64},{96,80},{112,96},{17,1},{33... | collective-permute-start | bytes 43016 | tf_op jit(solution)/shard_map/ppermute | solution.py:20
  (76 other events, 2264.0 us)
Sparse Core Ops, SparseCore 0:
  97.6 90.3 all-reduce.6
  312.4 87.1 all-reduce.8
where the time goes:
time: 457 us; the launch traced here: 448 us
  waiting for transfers between devices  151 us (33%)
  blocking collectives  118 us (26%)
  local copies, waits for them, and re-layouts  89.6 us (20%)
  other arithmetic  35.7 us (8%)
  starting transfers between devices  25.1 us (5%)
  between operations  15.4 us (3%)
  matrix products  12.7 us (3%)
    psum x2, waiting for transfers between devices, per_device(): hs_total = lax.psum(hs_part, 'band')  129 us
    all_to_all x2, blocking collectives, per_device(): lax.all_to_all(update, 'sub', split_axis=0, concat_axis=1, tiled=True)  64.9 us
    psum x1, blocking collectives, per_device(): combined = lax.psum(partial_map, 'band').astype(jnp.bfloat16)  35 us
    unnamed x190, local copies, waits for them, and re-layouts  31.5 us
    reshape x2, local copies, waits for them, and re-layouts, hs_gradient(): padded.reshape(bands, groups + 2, 4, columns + 2, 4)  22.2 us
    all_to_all x1, blocking collectives, per_device(): lax.all_to_all(current.astype(jnp.bfloat16), 'sub', split_axis=1, concat_...  18.5 us
    another operation x24, other arithmetic, hs_gradient(): outer.append(jnp.stack(inner, axis=1))  16.7 us
    pad x2, local copies, waits for them, and re-layouts, hs_gradient(): padded = jnp.pad(extended, ((0, 0), (0, 0), (4, 4)))  15 us
  transfers between devices with their start and end apart: 11, of which 7 were waited for; matrix products, arithmetic and copies ran while one was open for 4% of the time, Pallas kernels for 0%

commit v1 on v0

--- a/solution.py
+++ b/solution.py
@@ -94,7 +94,11 @@
             current.astype(jnp.bfloat16), "sub", split_axis=1, concat_axis=0, tiled=True
         )
         hs_part = hs_gradient(rounded, basis, kernels, hs_image)
-        hs_total = lax.psum(hs_part, "band")
+        hs_total = hs_part
+        for hop in (1, 2, 4, 8):
+            hs_total = hs_total + lax.ppermute(
+                hs_total, "band", [(dev, dev ^ hop) for dev in range(16)]
+            )
         update = step_scale * (hs_total + ms_gradient(rounded, ms_image, combined))
         current = current + lax.all_to_all(update, "sub", split_axis=0, concat_axis=1, tiled=True)
     return current

time: 457 us -> 650 us (1.42)
  waiting for transfers between devices: 151 us -> 346 us
  starting transfers between devices: 25.1 us -> 39.9 us
  between operations: 15.4 us -> 1.98 us
  other arithmetic: 35.7 us -> 42.2 us
    ppermute x0 -> x8, waiting for transfers between devices: none -> 324 us  [per_device(): lax.ppermute(hs_total, 'band', [(dev, dev ^ hop) for dev in range(16)])]
    psum x2 -> x0, waiting for transfers between devices: 129 us -> none  [per_device(): hs_total = lax.psum(hs_part, 'band')]
    ppermute x0 -> x8, starting transfers between devices: none -> 15 us  [per_device(): lax.ppermute(hs_total, 'band', [(dev, dev ^ hop) for dev in range(16)])]
  transfers between devices with their start and end apart: 11 -> 17, of which waited for: 7 -> 13; matrix products, arithmetic and copies ran while one was open for 4% -> 2% of each run, Pallas kernels for 0% -> 0%
where the time goes in v1:
time: 650 us; the launch traced here: 641 us
  waiting for transfers between devices  346 us (53%)
  blocking collectives  114 us (18%)
  local copies, waits for them, and re-layouts  83.5 us (13%)
  other arithmetic  42.2 us (6%)
  starting transfers between devices  39.9 us (6%)
  matrix products  12.8 us (2%)
    ppermute x8, waiting for transfers between devices, per_device(): lax.ppermute(hs_total, 'band', [(dev, dev ^ hop) for dev in range(16)])  324 us
    all_to_all x2, blocking collectives, per_device(): lax.all_to_all(update, 'sub', split_axis=0, concat_axis=1, tiled=True)  63.6 us
    psum x1, blocking collectives, per_device(): combined = lax.psum(partial_map, 'band').astype(jnp.bfloat16)  31.9 us
    unnamed x190, local copies, waits for them, and re-layouts  25.4 us
    reshape x2, local copies, waits for them, and re-layouts, hs_gradient(): padded.reshape(bands, groups + 2, 4, columns + 2, 4)  22.2 us
    all_to_all x1, blocking collectives, per_device(): lax.all_to_all(current.astype(jnp.bfloat16), 'sub', split_axis=1, concat_...  18.5 us
    another operation x24, other arithmetic, hs_gradient(): outer.append(jnp.stack(inner, axis=1))  16.3 us
    ppermute x8, starting transfers between devices, per_device(): lax.ppermute(hs_total, 'band', [(dev, dev ^ hop) for dev in range(16)])  15 us
  transfers between devices with their start and end apart: 17, of which 13 were waited for; matrix products, arithmetic and copies ran while one was open for 2% of the time, Pallas kernels for 0%

profile of v1, /device:TPU:1, one launch (start us, length us, event | category | flops | bytes accessed | tf_op | source)
XLA Modules:
  0.0 640.9 jit_solution(12551910427168771347)
XLA Ops:
  3.9 5.8 all-to-all-start
  13.0 11.8 %all-to-all-done = bf16[4,128,1024]{2,0,1:T(4,128)(2,1)S(1)} async-done(((bf16[4,128,1024]{2,0,1:T(4,128)(2,1)}), bf16[4,128,1024]{2,0,1:T(4,128)(2,1)S(1)}, u32[]{:S(2)}, u32[]{:S(2)}) %all-to-all-start) | async-done | bytes 1048608 | tf_op jit(solution)/shard_map/all_to_all | solution.py:93
  35.9 4.8 copy.442
  40.7 7.5 %pad.14.clone = bf16[14,24,1032]{0,2,1:T(8,128)(2,1)} pad(bf16[14,24,1024]{0,2,1:T(8,128)(2,1)} %copy.442, bf16[]{:T(256)} %constant.4.clone.1), padding=0_0x0_0x4_4 | pad | bytes 1381634 | tf_op jit(solution)/shard_map/jit(_pad)/pad | solution.py:37
  48.1 11.1 %copy.392 = bf16[14,6,4,258,4]{3,1,0,4,2:T(8,128)(2,1)S(1)} copy(bf16[14,6,4,258,4]{0,4,3,2,1:T(4,128)(2,1)} %bitcast.1051) | data formatting | bytes 1387008 | tf_op jit(solution)/shard_map/reshape | solution.py:38
  79.6 4.9 copy.413
  90.8 45.1 %collective-permute-done.4 = f32[32,16,1024]{2,1,0:T(8,128)S(1)} collective-permute-done((f32[32,16,1024]{2,1,0:T(8,128)S(1)}, f32[32,16,1024]{2,1,0:T(8,128)S(1)}, u32[]{:S(2)}, u32[]{:S(2)}) %collective-permute-start.4) | collective-permute-done | bytes 2097184 | tf_op jit(solution)/shard_map/ppermute | solution.py:99
  139.4 46.1 %collective-permute-done.5 = f32[32,16,1024]{2,1,0:T(8,128)S(1)} collective-permute-done((f32[32,16,1024]{2,1,0:T(8,128)S(1)}, f32[32,16,1024]{2,1,0:T(8,128)S(1)}, u32[]{:S(2)}, u32[]{:S(2)}) %collective-permute-start.5) | collective-permute-done | bytes 2097184 | tf_op jit(solution)/shard_map/ppermute | solution.py:99
  187.8 45.4 %collective-permute-done.6 = f32[32,16,1024]{2,1,0:T(8,128)S(1)} collective-permute-done((f32[32,16,1024]{2,1,0:T(8,128)S(1)}, f32[32,16,1024]{2,1,0:T(8,128)S(1)}, u32[]{:S(2)}, u32[]{:S(2)}) %collective-permute-start.6) | collective-permute-done | bytes 2097184 | tf_op jit(solution)/shard_map/ppermute | solution.py:99
  238.6 31.9 %psum.7 = bf16[8,32]{1,0:T(8,128)(2,1)S(1)} all-reduce(f32[8,32]{1,0:T(8,128)S(1)} %fusion.213), channel_id=1, replica_groups=mesh['sub'=8,'band'=16] {'band'}, use_global_device_ids=true, to_apply=%region_0.0 | all-reduce | flops 256 | bytes 1536 | tf_op jit(solution)/shard_map/psum | solution.py:90
  275.2 8.6 %collective-permute-done.7 = f32[32,16,1024]{2,1,0:T(8,128)} collective-permute-done((f32[32,16,1024]{2,1,0:T(8,128)}, f32[32,16,1024]{2,1,0:T(8,128)}, u32[]{:S(2)}, u32[]{:S(2)}) %collective-permute-start.7) | collective-permute-done | bytes 2097184 | tf_op jit(solution)/shard_map/ppermute | solution.py:99
  286.7 31.7 %all_to_all.66 = f32[32,16,1024]{2,1,0:T(8,128)S(1)} all-to-all(f32[32,16,1024]{2,1,0:T(8,128)S(1)} %fusion.3), channel_id=1, replica_groups=mesh['sub'=8,'band'=16] {'sub'}, dimensions={0} | all-to-all | bytes 4194304 | tf_op jit(solution)/shard_map/all_to_all | solution.py:103
  321.8 18.5 %all_to_all.67 = bf16[4,128,1024]{2,0,1:T(4,128)(2,1)S(1)} all-to-all(bf16[4,128,1024]{2,0,1:T(4,128)(2,1)S(1)} %fusion.6), channel_id=1, replica_groups=mesh['sub'=8,'band'=16] {'sub'}, dimensions={1} | all-to-all | bytes 2097152 | tf_op jit(solution)/shard_map/all_to_all | solution.py:93
  348.0 4.1 collective-permute-done.9
  352.5 4.8 copy.443
  357.3 7.5 %pad.16.clone = bf16[14,24,1032]{0,2,1:T(8,128)(2,1)} pad(bf16[14,24,1024]{0,2,1:T(8,128)(2,1)} %copy.443, bf16[]{:T(256)} %constant.4.clone.1), padding=0_0x0_0x4_4 | pad | bytes 1381634 | tf_op jit(solution)/shard_map/jit(_pad)/pad | solution.py:37
  364.7 11.1 %copy.418 = bf16[14,6,4,258,4]{3,1,0,4,2:T(8,128)(2,1)S(1)} copy(bf16[14,6,4,258,4]{0,4,3,2,1:T(4,128)(2,1)} %bitcast.1050) | data formatting | bytes 1387008 | tf_op jit(solution)/shard_map/reshape | solution.py:38
  376.1 4.2 convert_subtract_fusion
  397.0 4.9 copy.439
  407.4 45.9 %collective-permute-done.12 = f32[32,16,1024]{2,1,0:T(8,128)S(1)} collective-permute-done((f32[32,16,1024]{2,1,0:T(8,128)S(1)}, f32[32,16,1024]{2,1,0:T(8,128)S(1)}, u32[]{:S(2)}, u32[]{:S(2)}) %collective-permute-start.12) | collective-permute-done | bytes 2097184 | tf_op jit(solution)/shard_map/ppermute | solution.py:99
  455.9 47.0 %collective-permute-done.13 = f32[32,16,1024]{2,1,0:T(8,128)S(1)} collective-permute-done((f32[32,16,1024]{2,1,0:T(8,128)S(1)}, f32[32,16,1024]{2,1,0:T(8,128)S(1)}, u32[]{:S(2)}, u32[]{:S(2)}) %collective-permute-start.13) | collective-permute-done | bytes 2097184 | tf_op jit(solution)/shard_map/ppermute | solution.py:99
  503.7 46.5 %collective-permute-done.14 = f32[32,16,1024]{2,1,0:T(8,128)S(1)} collective-permute-done((f32[32,16,1024]{2,1,0:T(8,128)S(1)}, f32[32,16,1024]{2,1,0:T(8,128)S(1)}, u32[]{:S(2)}, u32[]{:S(2)}) %collective-permute-start.14) | collective-permute-done | bytes 2097184 | tf_op jit(solution)/shard_map/ppermute | solution.py:99
  560.5 39.0 %collective-permute-done.15 = f32[32,16,1024]{2,1,0:T(8,128)} collective-permute-done((f32[32,16,1024]{2,1,0:T(8,128)}, f32[32,16,1024]{2,1,0:T(8,128)}, u32[]{:S(2)}, u32[]{:S(2)}) %collective-permute-start.15) | collective-permute-done | bytes 2097184 | tf_op jit(solution)/shard_map/ppermute | solution.py:99
  602.4 31.9 %all_to_all.68 = f32[32,16,1024]{2,1,0:T(8,128)S(1)} all-to-all(f32[32,16,1024]{2,1,0:T(8,128)S(1)} %fusion.2), channel_id=1, replica_groups=mesh['sub'=8,'band'=16] {'sub'}, dimensions={0} | all-to-all | bytes 4194304 | tf_op jit(solution)/shard_map/all_to_all | solution.py:103
  (282 shorter events, 118.8 us)
Async XLA Ops:
  3.9 20.9 %all-to-all-start = ((bf16[4,128,1024]{2,0,1:T(4,128)(2,1)}), bf16[4,128,1024]{2,0,1:T(4,128)(2,1)S(1)}, u32[]{:S(2)}, u32[]{:S(2)}) async-start(bf16[4,128,1024]{2,0,1:T(4,128)(2,1)} %copy.459), calls=%async_computation | async-start | bytes 2097152 | tf_op jit(solution)/shard_map/all_to_all | solution.py:93
  10.7 66.1 %copy-start.22 = (f32[14]{0:T(128)}, f32[14]{0:T(128)S(1)}, u32[]{:S(2)}) copy-start(f32[14]{0:T(128)S(1)} %get-tuple-element.23) | copy-start | bytes 172
  11.9 66.6 %copy-start.24 = (f32[14]{0:T(128)}, f32[14]{0:T(128)S(1)}, u32[]{:S(2)}) copy-start(f32[14]{0:T(128)S(1)} %get-tuple-element.27) | copy-start | bytes 172
  11.9 66.6 %copy-start.26 = (f32[14]{0:T(128)}, f32[14]{0:T(128)S(1)}, u32[]{:S(2)}) copy-start(f32[14]{0:T(128)S(1)} %get-tuple-element.31) | copy-start | bytes 172
  11.9 66.8 %copy-start.12 = (f32[14]{0:T(128)}, f32[14]{0:T(128)S(1)}, u32[]{:S(2)}) copy-start(f32[14]{0:T(128)S(1)} %get-tuple-element.26) | copy-start | bytes 172
  11.9 66.8 %copy-start.14 = (f32[14]{0:T(128)}, f32[14]{0:T(128)S(1)}, u32[]{:S(2)}) copy-start(f32[14]{0:T(128)S(1)} %get-tuple-element.30) | copy-start | bytes 172
  13.0 65.7 %copy-start.28 = (f32[14]{0:T(128)}, f32[14]{0:T(128)S(1)}, u32[]{:S(2)}) copy-start(f32[14]{0:T(128)S(1)} %get-tuple-element.52) | copy-start | bytes 172
  13.0 65.7 %copy-start.30 = (f32[14]{0:T(128)}, f32[14]{0:T(128)S(1)}, u32[]{:S(2)}) copy-start(f32[14]{0:T(128)S(1)} %get-tuple-element.56) | copy-start | bytes 172
  26.5 6.8 %collective-permute-start = (bf16[14,4,1024]{2,1,0:T(4,128)(2,1)S(1)}, bf16[14,4,1024]{2,1,0:T(4,128)(2,1)S(1)}, u32[]{:S(2)}, u32[]{:S(2)}) collective-permute-start(bf16[14,4,1024]{2,1,0:T(4,128)(2,1)S(1)} %get-tuple-element.88), channel_id=1, source_target_pairs={{0,16},{16,32},{32,48},{48,64},{64,80},{80,96},{96,112},{1,17},{17... | collective-permute-start | bytes 344072 | tf_op jit(solution)/shard_map/ppermute | solution.py:18
  29.4 6.1 collective-permute-start.1
  63.1 4.5 collective-permute-start.2
  65.0 5.0 collective-permute-start.3
  89.4 46.4 %collective-permute-start.4 = (f32[32,16,1024]{2,1,0:T(8,128)S(1)}, f32[32,16,1024]{2,1,0:T(8,128)S(1)}, u32[]{:S(2)}, u32[]{:S(2)}) collective-permute-start(f32[32,16,1024]{2,1,0:T(8,128)S(1)} %bitcast.1060), channel_id=1, source_target_pairs={{0,1},{1,0},{2,3},{3,2},{4,5},{5,4},{6,7},{7,6},{8,9},{9,8},{10,11... | collective-permute-start | bytes 6291464 | tf_op jit(solution)/shard_map/ppermute | solution.py:99
  136.4 49.1 %collective-permute-start.5 = (f32[32,16,1024]{2,1,0:T(8,128)S(1)}, f32[32,16,1024]{2,1,0:T(8,128)S(1)}, u32[]{:S(2)}, u32[]{:S(2)}) collective-permute-start(f32[32,16,1024]{2,1,0:T(8,128)S(1)} %bitcast_add_fusion.5), channel_id=1, source_target_pairs={{0,2},{1,3},{2,0},{3,1},{4,6},{5,7},{6,4},{7,5},{8,10},{9,11},{10,... | collective-permute-start | bytes 6291464 | tf_op jit(solution)/shard_map/ppermute | solution.py:99
  186.0 47.1 %collective-permute-start.6 = (f32[32,16,1024]{2,1,0:T(8,128)S(1)}, f32[32,16,1024]{2,1,0:T(8,128)S(1)}, u32[]{:S(2)}, u32[]{:S(2)}) collective-permute-start(f32[32,16,1024]{2,1,0:T(8,128)S(1)} %add.1062), channel_id=1, source_target_pairs={{0,4},{1,5},{2,6},{3,7},{4,0},{5,1},{6,2},{7,3},{8,12},{9,13},{10,... | collective-permute-start | bytes 6291464 | tf_op jit(solution)/shard_map/ppermute | solution.py:99
  234.9 48.9 %collective-permute-start.7 = (f32[32,16,1024]{2,1,0:T(8,128)}, f32[32,16,1024]{2,1,0:T(8,128)}, u32[]{:S(2)}, u32[]{:S(2)}) collective-permute-start(f32[32,16,1024]{2,1,0:T(8,128)} %add.1063), channel_id=1, source_target_pairs={{0,8},{1,9},{2,10},{3,11},{4,12},{5,13},{6,14},{7,15},{8,0},{9,1},... | collective-permute-start | bytes 6291464 | tf_op jit(solution)/shard_map/ppermute | solution.py:99
  342.9 5.1 collective-permute-start.8
  346.0 6.1 collective-permute-start.9
  380.5 4.8 collective-permute-start.10
  382.4 5.0 collective-permute-start.11
  406.8 46.4 %collective-permute-start.12 = (f32[32,16,1024]{2,1,0:T(8,128)S(1)}, f32[32,16,1024]{2,1,0:T(8,128)S(1)}, u32[]{:S(2)}, u32[]{:S(2)}) collective-permute-start(f32[32,16,1024]{2,1,0:T(8,128)S(1)} %bitcast.1061), channel_id=1, source_target_pairs={{0,1},{1,0},{2,3},{3,2},{4,5},{5,4},{6,7},{7,6},{8,9},{9,8},{10,11... | collective-permute-start | bytes 6291464 | tf_op jit(solution)/shard_map/ppermute | solution.py:99
  453.8 49.1 %collective-permute-start.13 = (f32[32,16,1024]{2,1,0:T(8,128)S(1)}, f32[32,16,1024]{2,1,0:T(8,128)S(1)}, u32[]{:S(2)}, u32[]{:S(2)}) collective-permute-start(f32[32,16,1024]{2,1,0:T(8,128)S(1)} %bitcast_add_fusion.4), channel_id=1, source_target_pairs={{0,2},{1,3},{2,0},{3,1},{4,6},{5,7},{6,4},{7,5},{8,10},{9,11},{10,... | collective-permute-start | bytes 6291464 | tf_op jit(solution)/shard_map/ppermute | solution.py:99
  503.5 46.7 %collective-permute-start.14 = (f32[32,16,1024]{2,1,0:T(8,128)S(1)}, f32[32,16,1024]{2,1,0:T(8,128)S(1)}, u32[]{:S(2)}, u32[]{:S(2)}) collective-permute-start(f32[32,16,1024]{2,1,0:T(8,128)S(1)} %add.1213), channel_id=1, source_target_pairs={{0,4},{1,5},{2,6},{3,7},{4,0},{5,1},{6,2},{7,3},{8,12},{9,13},{10,... | collective-permute-start | bytes 6291464 | tf_op jit(solution)/shard_map/ppermute | solution.py:99
  552.0 47.5 %collective-permute-start.15 = (f32[32,16,1024]{2,1,0:T(8,128)}, f32[32,16,1024]{2,1,0:T(8,128)}, u32[]{:S(2)}, u32[]{:S(2)}) collective-permute-start(f32[32,16,1024]{2,1,0:T(8,128)} %add.1214), channel_id=1, source_target_pairs={{0,8},{1,9},{2,10},{3,11},{4,12},{5,13},{6,14},{7,15},{8,0},{9,1},... | collective-permute-start | bytes 6291464 | tf_op jit(solution)/shard_map/ppermute | solution.py:99
  (82 other events, 2800.2 us)
